TPU v7x, 32 devices: a whole 2x2x4 slice. The times are simulated.
32 devices in a mesh: dom: 2 (over y), exp: 16 (over z, x, core).
Axes of the slice: x: 2, y: 2, z: 4, core: 2. Of those that a mesh axis runs over, the one named last changes fastest.
Arguments:
- queries: bfloat16 [128, 4096], P(('dom', 'exp')), parts along dimension 0
- new_keys: bfloat16 [128, 1024], P(('dom', 'exp')), parts along dimension 0, may hold values from -6 to 6
- new_values: bfloat16 [128, 1024], P(('dom', 'exp')), parts along dimension 0, may hold values from -6 to 6
- cache_keys: bfloat16 [128, 32, 1024], P(('dom', 'exp')), parts along dimension 0
- cache_values: bfloat16 [128, 32, 1024], P(('dom', 'exp')), parts along dimension 0, may hold values from -6 to 6
- lengths: int32 [128], P(('dom', 'exp')), parts along dimension 0, may hold values from 2 to 32, as said below
- norm_gain: float32 [4096], replicated, may hold values from 0.5 to 1.5
- route_ids: int32 [128, 2], P(('dom', 'exp')), parts along dimension 0, may hold values from 0 to 7, all different within a row; in each aligned block of 4 rows (0 to 3, 4 to 7, ...) at most 2 rows name the same one
- route_weights: float32 [128, 2], P(('dom', 'exp')), parts along dimension 0, may hold values from 0.1 to 1
- active_blocks: int32 [16, 64], P('dom'), parts along dimension 0, may hold values 0 or 1
- gate_weight: bfloat16 [65536, 4096], P('exp'), may hold values from -0.09375 to 0.09375
- up_weight: bfloat16 [65536, 4096], P('exp'), may hold values from -0.09375 to 0.09375
- down_weight: bfloat16 [65536, 4096], P('exp'), may hold values from -0.1875 to 0.1875
Outputs:
- attended: bfloat16 [128, 4096], P(('dom', 'exp')), parts along dimension 0
- expert_out: bfloat16 [128, 4096], P(('dom', 'exp')), parts along dimension 0
There are 2 independent parts, one for each index of `dom`. A program takes and returns all parts, laid end to end along the dimension named above; an argument that names none is the same for every part. Nothing has to cross between parts.
Inputs may be any that keep to these rules, and one draw needn't show every extreme that they name: `lengths`: the first row of the group has 32 positions in use. `route_ids`: among the rows of one device no expert is named by more than 2 rows, a bound that some block reaches.
All inputs are finite; a program needn't handle non-finite values.
Results may differ from a plain program's by a relative error of at most 0.014.
Values may be sent and summed in bfloat16 or wider, within the bound.
No kernel may reach another device: no remote copies, remote signals or barrier semaphores. Data moves between devices by JAX's collectives and lax.ppermute only.
A program may use at most 192 MiB of HBM per device.

v0:
```python
import math

import jax
import jax.numpy as jnp
from jax import lax
from jax.experimental import pallas as pl
from jax.experimental.pallas import tpu as pltpu
from jax.sharding import PartitionSpec as P

KV_HEADS = 8
BLOCK = 128
CAP = 2
EPSILON = 1e-05

QUAD = 4 * BLOCK
SLOTS = 8

FWD16 = False
RET16 = False

vmem = pl.BlockSpec(memory_space=pltpu.VMEM)
smem = pl.BlockSpec(memory_space=pltpu.SMEM)
hbm = pl.BlockSpec(memory_space=pl.ANY)


def slot_of(ids_ref, row, choice):
    mine = ids_ref[choice, row]
    rank = jnp.int32(0)
    for r in range(row + 1):
        for k in range(2):
            if (r, k) < (row, choice):
                rank += (ids_ref[k, r] == mine).astype(jnp.int32)
    return mine * CAP + rank


def attend_kernel(
    lengths_ref,
    ids_ref,
    route_weights_ref,
    flags_ref,
    queries_ref,
    new_keys_ref,
    new_values_ref,
    keys_ref,
    values_ref,
    gain_ref,
    attended_ref,
    outgoing_ref,
    mix_ref,
    list_ref,
):
    rows, width = queries_ref.shape
    context = keys_ref.shape[1]
    head_size = new_keys_ref.shape[1] // KV_HEADS
    group = width // head_size // KV_HEADS
    spots = rows * context
    stack = group * rows
    scale = head_size ** (-0.5)
    list_blocks(flags_ref, list_ref, list_ref.shape[1] - 1)
    query = queries_ref[...].astype(jnp.float32)
    new_key = new_keys_ref[...].astype(jnp.float32)
    new_value = new_values_ref[...].astype(jnp.float32)

    scores, owns = [], []
    for j in range(KV_HEADS):
        columns = slice(j * head_size, (j + 1) * head_size)
        heads = [query[:, (j * group + g) * head_size : (j * group + g + 1) * head_size] for g in range(group)]
        stacked = jnp.concatenate(heads, axis=0)
        keys = keys_ref[:, :, columns].reshape(spots, head_size)
        scores.append(
            lax.dot_general(
                stacked.astype(jnp.bfloat16), keys, (((1,), (1,)), ((), ())), preferred_element_type=jnp.float32
            )
        )
        own_key = jnp.concatenate([new_key[:, columns]] * group, axis=0)
        owns.append(jnp.sum(stacked * own_key, axis=1, keepdims=True))
    score = jnp.concatenate(scores, axis=0) * scale
    own = jnp.concatenate(owns, axis=0) * scale
    row_of_line = lax.broadcasted_iota(jnp.int32, score.shape, 0) % rows
    spot = lax.broadcasted_iota(jnp.int32, score.shape, 1)
    valid = jnp.zeros(score.shape, jnp.bool_)
    for r in range(rows):
        valid = valid | ((row_of_line == r) & (spot >= r * context) & (spot < r * context + lengths_ref[r]))
    score = jnp.where(valid, score, -jnp.inf)
    top = jnp.maximum(jnp.max(score, axis=1, keepdims=True), own)
    score_exp = jnp.exp(score - top)
    own_exp = jnp.exp(own - top)
    denominator = jnp.sum(score_exp, axis=1, keepdims=True) + own_exp
    prob = (score_exp / denominator).astype(jnp.bfloat16)
    own_prob = (own_exp / denominator).astype(jnp.bfloat16).astype(jnp.float32)

    pieces = []
    for j in range(KV_HEADS):
        columns = slice(j * head_size, (j + 1) * head_size)
        lines = slice(j * stack, (j + 1) * stack)
        values = values_ref[:, :, columns].reshape(spots, head_size)
        mixture = jnp.dot(prob[lines], values, preferred_element_type=jnp.float32)
        own_value = jnp.concatenate([new_value[:, columns]] * group, axis=0)
        mixture = mixture + own_prob[lines] * own_value
        pieces += [mixture[g * rows : (g + 1) * rows] for g in range(group)]
    attended = jnp.concatenate(pieces, axis=1).astype(jnp.bfloat16)
    attended_ref[...] = attended

    features = attended.astype(jnp.float32)
    mean_square = jnp.mean(features * features, axis=1, keepdims=True)
    normed = features * lax.rsqrt(mean_square + EPSILON) * gain_ref[...]
    normed = normed.astype(jnp.bfloat16).astype(jnp.float32)
    places = outgoing_ref.shape[0]
    experts = flags_ref.shape[0]
    line = lax.broadcasted_iota(jnp.int32, (experts * CAP, 1), 0)
    mix_row = lax.broadcasted_iota(jnp.int32, mix_ref.shape, 0)
    mix_slot = lax.broadcasted_iota(jnp.int32, mix_ref.shape, 1)
    packed = jnp.zeros((experts * CAP, width), jnp.float32)
    mix = jnp.zeros(mix_ref.shape, jnp.float32)
    for r in range(rows):
        slots = [slot_of(ids_ref, r, k) for k in range(2)]
        packed = packed + jnp.where((line == slots[0]) | (line == slots[1]), normed[r : r + 1, :], 0.0)
        for k in range(2):
            mix = mix + jnp.where((mix_row == r) & (mix_slot == slots[k]), route_weights_ref[k, r], 0.0)
    packed = packed.astype(jnp.bfloat16)
    for place in range(places):
        expert = place // (places // experts)
        outgoing_ref[place] = packed[expert * CAP : (expert + 1) * CAP, :]
    mix_ref[...] = mix


def list_blocks(flags_ref, list_ref, blocks):
    experts = flags_ref.shape[0]
    groups = lax.axis_size("exp") // experts
    position = lax.axis_index("exp")
    expert = position // groups
    first = (position % groups) * blocks

    count = jnp.int32(0)
    for b in range(blocks):
        list_ref[0, count] = b
        count += (flags_ref[expert, first + b] != 0).astype(jnp.int32)
    list_ref[0, blocks] = count


def item_copies(item, count, list_ref, weights, ring_ref, sems):
    gate_ref, up_ref, down_ref = weights
    pairs = (count + 1) // 2
    slot = item % ring_ref.shape[0]

    def copy(source_ref, position, part):
        rows = pl.ds(pl.multiple_of(list_ref[0, position] * BLOCK, BLOCK), BLOCK)
        return pltpu.make_async_copy(
            source_ref.at[rows, :], ring_ref.at[slot, pl.ds(part * BLOCK, BLOCK), :], sems.at[slot, part]
        )

    def apply(act):
        @pl.when(item < pairs)
        def _():
            for s in range(2):
                @pl.when(2 * item + s < count)
                def _():
                    act(copy(gate_ref, 2 * item + s, 2 * s))
                    act(copy(up_ref, 2 * item + s, 2 * s + 1))

        @pl.when(item >= pairs)
        def _():
            for s in range(2):
                position = 2 * (item - pairs) + s
                @pl.when(position < count)
                def _():
                    act(copy(down_ref, position, s))

    return apply


def experts_kernel(
    list_ref,
    near_ref,
    far_ref,
    attended_ref,
    gate_ref,
    up_ref,
    down_ref,
    keep_ref,
    give_ref,
    attended_out,
    ring_ref,
    x_ref,
    hidden_ref,
    total_ref,
    sems,
    attended_sem,
):
    blocks = gate_ref.shape[0] // BLOCK
    core = lax.axis_index("exp") % 2
    chips = x_ref.shape[0] // (2 * CAP)
    half = chips * CAP
    ring_slots = ring_ref.shape[0]
    count = list_ref[0, blocks]
    weights = (gate_ref, up_ref, down_ref)
    whole = count // 2
    pairs = (count + 1) // 2

    def start(item, carry):
        item_copies(item, count, list_ref, weights, ring_ref, sems)(lambda copy: copy.start())
        return carry

    def settle(item):
        item_copies(item, count, list_ref, weights, ring_ref, sems)(lambda copy: copy.wait())

    lax.fori_loop(0, ring_slots, start, 0)
    write = pltpu.make_async_copy(attended_ref, attended_out, attended_sem)
    write.start()
    for chip in range(chips):
        x_ref[chip * CAP : (chip + 1) * CAP, :] = near_ref[2 * chip + core] if FWD16 else near_ref[chip]
        x_ref[half + chip * CAP : half + (chip + 1) * CAP, :] = near_ref[2 * chip + 1 - core] if FWD16 else far_ref[chip]
    total_ref[...] = jnp.zeros_like(total_ref)

    def project(item, number):
        settle(item)
        slot = item % ring_slots
        both = lax.dot_general(
            ring_ref[slot, : 2 * number * BLOCK, :],
            x_ref[...],
            (((1,), (1,)), ((), ())),
            preferred_element_type=jnp.float32,
        )
        for s in range(number):
            gate = both[2 * s * BLOCK : (2 * s + 1) * BLOCK]
            up = both[(2 * s + 1) * BLOCK : (2 * s + 2) * BLOCK]
            hidden = (jax.nn.relu(gate) * jax.nn.relu(up)).T
            hidden_ref[item, :, s * BLOCK : (s + 1) * BLOCK] = hidden.astype(jnp.bfloat16)
        start(item + ring_slots, 0)

    def contract(chunk, number):
        item = pairs + chunk
        settle(item)
        total_ref[...] += jnp.dot(
            hidden_ref[chunk, :, : number * BLOCK],
            ring_ref[item % ring_slots, : number * BLOCK, :],
            preferred_element_type=jnp.float32,
        )
        start(item + ring_slots, 0)

    def steps(body):
        def pair(step, carry):
            body(step, 2)
            return carry

        lax.fori_loop(0, whole, pair, 0)

        @pl.when(whole < pairs)
        def _():
            body(whole, 1)

    steps(project)
    steps(contract)
    if RET16:
        for chip in range(chips):
            give_ref[2 * chip + core] = total_ref[chip * CAP : (chip + 1) * CAP, :].astype(jnp.bfloat16)
            give_ref[2 * chip + 1 - core] = total_ref[half + chip * CAP : half + (chip + 1) * CAP, :].astype(jnp.bfloat16)
    else:
        keep_ref[...] = total_ref[0:half, :]
        give_ref[...] = total_ref[half:, :].astype(jnp.bfloat16)
    write.wait()


def merge_kernel(keep_ref, taken_ref, out_ref):
    total = (keep_ref[...] + taken_ref[...].astype(jnp.float32)).astype(jnp.bfloat16)
    for chip in range(out_ref.shape[0]):
        out_ref[chip] = total[chip * CAP : (chip + 1) * CAP, :]


def combine_kernel(mix_ref, returned_ref, out_ref):
    rows = out_ref.shape[0]
    experts = mix_ref.shape[1] // CAP
    share = returned_ref.shape[0] // experts
    mix = mix_ref[...]
    total = jnp.zeros(out_ref.shape, jnp.float32)
    for expert in range(experts):
        value = returned_ref[expert * share].astype(jnp.float32)
        for part in range(1, share):
            value = value + returned_ref[expert * share + part].astype(jnp.float32)
        for c in range(CAP):
            slot = expert * CAP + c
            total = total + mix[0:rows, slot : slot + 1] * value[c : c + 1, :]
    out_ref[...] = total.astype(jnp.bfloat16)


def ring_of(gate_weight):
    blocks, width = gate_weight.shape[0] // BLOCK, gate_weight.shape[1]
    slots = min(SLOTS, (blocks + 1) // 2 * 2)
    return blocks, (slots, QUAD, width)


def in_vmem(array):
    return pltpu.with_memory_space_constraint(array, pltpu.VMEM)


def experts(listing, near, far, attended, gate_weight, up_weight, down_weight):
    blocks, ring_shape = ring_of(gate_weight)
    half, width = lax.axis_size("exp") // 2 * CAP, near.shape[2]
    return pl.pallas_call(
        experts_kernel,
        out_shape=(
            pltpu.VMEM((8, 128) if RET16 else (half, width), jnp.float32),
            pltpu.VMEM((half, CAP, width) if RET16 else (half, width), jnp.bfloat16),
            jax.ShapeDtypeStruct(attended.shape, jnp.bfloat16),
        ),
        in_specs=[smem, vmem, vmem, vmem, hbm, hbm, hbm],
        out_specs=(vmem, vmem, hbm),
        scratch_shapes=[
            pltpu.VMEM(ring_shape, jnp.bfloat16),
            pltpu.VMEM((2 * half, width), jnp.bfloat16),
            pltpu.VMEM(((blocks + 1) // 2, 2 * half, 2 * BLOCK), jnp.bfloat16),
            pltpu.VMEM((2 * half, width), jnp.float32),
            pltpu.SemaphoreType.DMA((ring_shape[0], 4)),
            pltpu.SemaphoreType.DMA,
        ],
        compiler_params=pltpu.CompilerParams(vmem_limit_bytes=6 * 2**20 + 16 * half * width + 2 * math.prod(ring_shape)),
        name="experts",
    )(pltpu.with_memory_space_constraint(listing, pltpu.SMEM), in_vmem(near), in_vmem(far), in_vmem(attended), gate_weight, up_weight, down_weight)


def shards(
    queries,
    new_keys,
    new_values,
    cache_keys,
    cache_values,
    lengths,
    norm_gain,
    route_ids,
    route_weights,
    active_blocks,
    gate_weight,
    up_weight,
    down_weight,
):
    devices = lax.axis_size("exp")
    chips = devices // 2
    width = queries.shape[1]
    half = chips * CAP
    same_core = [[2 * chip + core for chip in range(chips)] for core in range(2)]
    core_swap = [(device, device ^ 1) for device in range(devices)]

    experts_number = active_blocks.shape[0]
    attended, outgoing, mix, listing = pl.pallas_call(
        attend_kernel,
        out_shape=(
            pltpu.VMEM(queries.shape, jnp.bfloat16),
            pltpu.VMEM((devices if FWD16 else chips, CAP, width), jnp.bfloat16),
            pltpu.VMEM((8, experts_number * CAP), jnp.float32),
            pltpu.SMEM((1, gate_weight.shape[0] // BLOCK + 1), jnp.int32),
        ),
        in_specs=[smem] * 4 + [vmem] * 6,
        out_specs=(vmem, vmem, vmem, smem),
        name="attend",
    )(
        lengths,
        route_ids.T,
        route_weights.T,
        active_blocks,
        queries,
        new_keys,
        new_values,
        cache_keys,
        cache_values,
        norm_gain[None, :],
    )

    def exchange(array):
        return lax.all_to_all(array, "exp", split_axis=0, concat_axis=0, tiled=True, axis_index_groups=same_core)

    if FWD16:
        near = lax.all_to_all(outgoing, "exp", split_axis=0, concat_axis=0, tiled=True)
        far = near
    else:
        near = exchange(outgoing)
        far = lax.ppermute(near, "exp", core_swap)
    keep, give, attended = experts(listing, near, far, attended, gate_weight, up_weight, down_weight)
    if RET16:
        returned = lax.all_to_all(give, "exp", split_axis=0, concat_axis=0, tiled=True)
    else:
        taken = lax.ppermute(give, "exp", core_swap)
        merged = pl.pallas_call(
            merge_kernel,
            out_shape=pltpu.VMEM((chips, CAP, width), jnp.bfloat16),
            in_specs=[vmem, vmem],
            out_specs=vmem,
            name="merge",
        )(in_vmem(keep), in_vmem(taken))
        returned = exchange(merged)
    expert_out = pl.pallas_call(
        combine_kernel,
        out_shape=jax.ShapeDtypeStruct(queries.shape, jnp.bfloat16),
        in_specs=[vmem, vmem],
        out_specs=vmem,
        name="combine",
    )(in_vmem(mix), in_vmem(returned))
    return attended, expert_out


def solution(mesh):
    rows = P(("dom", "exp"), None)
    return jax.shard_map(
        shards,
        mesh=mesh,
        in_specs=(
            rows,
            rows,
            rows,
            P(("dom", "exp"), None, None),
            P(("dom", "exp"), None, None),
            P(("dom", "exp")),
            P(),
            rows,
            rows,
            P("dom", None),
            P("exp", None),
            P("exp", None),
            P("exp", None),
        ),
        out_specs=(rows, rows),
        check_vma=False,
    )
```

profile of v0, /device:TPU:0, one launch (start us, length us, event | category | flops | bytes accessed | tf_op | source)
XLA Modules:
  0.0 50.2 jit_solution(6004161585403747784)
XLA Ops:
  0.6 2.1 %attend.1 = (bf16[4,4096]{1,0:T(4,128)(2,1)S(1)}, bf16[8,2,4096]{2,1,0:T(2,128)(2,1)S(1)}, f32[8,16]{1,0:T(8,128)S(1)}, s32[1,33]{1,0:T(1,128)S(4)}) custom-call(s32[4]{0:T(128)} %lengths_ref.1, s32[2,4]{1,0:T(2,128)} %bitcast.4, f32[2,4]{1,0:T(2,128)} %bitcast.5, s32[8,64]{1,0:T(8,128)} %flags_ref.1, bf16[4,4096]{1,0:T(4,128)(2,1)} %queries_ref.1, ...), custom_call_target="tpu_custom_call" | custom-call | tf_op jit(solution)/shard_map/attend/pallas_call | solution.py:344
  2.7 14.4 %all_to_all.10.near_ref = bf16[8,2,4096]{2,1,0:T(2,128)(2,1)S(1)} all-to-all(bf16[8,2,4096]{2,1,0:T(2,128)(2,1)S(1)} %get-tuple-element.10), channel_id=1, replica_groups={{0,2,4,6,8,10,12,14},{1,3,5,7,9,11,13,15},{16,18,20,22,24,26,28,30},{17..., dimensions={0} | all-to-all | bytes 262144 | tf_op jit(solution)/shard_map/all_to_all | solution.py:369
  17.1 0.0 collective-permute-start
  17.1 1.3 %collective-permute-done.far_ref = bf16[8,2,4096]{2,1,0:T(2,128)(2,1)S(1)} collective-permute-done((bf16[8,2,4096]{2,1,0:T(2,128)(2,1)S(1)}, bf16[8,2,4096]{2,1,0:T(2,128)(2,1)S(1)}, u32[]{:S(2)}, u32[]{:S(2)}) %collective-permute-start) | collective-permute-done | bytes 131104 | tf_op jit(solution)/shard_map/ppermute | solution.py:376
  18.4 19.4 %experts.1 = (f32[16,4096]{1,0:T(8,128)S(1)}, bf16[16,4096]{1,0:T(8,128)(2,1)S(1)}, bf16[4,4096]{1,0:T(4,128)(2,1)}) custom-call(s32[1,33]{1,0:T(1,128)S(4)} %get-tuple-element.9.list_ref, bf16[8,2,4096]{2,1,0:T(2,128)(2,1)S(1)} %all_to_all.10.near_ref, bf16[8,2,4096]{2,1,0:T(2,128)(2,1)S(1)} %collective-permute-done.far_ref, ...), custom_call_target="tpu_custom_call" | custom-call | tf_op jit(solution)/shard_map/experts/pallas_call | solution.py:299
  37.8 0.1 collective-permute-start.1
  37.9 1.3 %collective-permute-done.1.taken_ref = bf16[16,4096]{1,0:T(8,128)(2,1)S(1)} collective-permute-done((bf16[16,4096]{1,0:T(8,128)(2,1)S(1)}, bf16[16,4096]{1,0:T(8,128)(2,1)S(1)}, u32[]{:S(2)}, u32[]{:S(2)}) %collective-permute-start.1) | collective-permute-done | bytes 131104 | tf_op jit(solution)/shard_map/ppermute | solution.py:381
  39.3 10.0 %all_to_all.11.returned_ref = bf16[8,2,4096]{2,1,0:T(2,128)(2,1)S(1)} all-to-all(bf16[8,2,4096]{2,1,0:T(2,128)(2,1)S(1)} %merge.1), channel_id=1, replica_groups={{0,2,4,6,8,10,12,14},{1,3,5,7,9,11,13,15},{16,18,20,22,24,26,28,30},{17..., dimensions={0} | all-to-all | bytes 262144 | tf_op jit(solution)/shard_map/all_to_all | solution.py:369
  49.2 1.0 %combine.1 = bf16[4,4096]{1,0:T(4,128)(2,1)} custom-call(f32[8,16]{1,0:T(8,128)S(1)} %get-tuple-element.13.mix_ref, bf16[8,2,4096]{2,1,0:T(2,128)(2,1)S(1)} %all_to_all.11.returned_ref), custom_call_target="tpu_custom_call" | custom-call | tf_op jit(solution)/shard_map/combine/pallas_call | solution.py:390
  (1 shorter events, 0.0 us)
Async XLA Ops:
  17.1 1.3 %collective-permute-start = (bf16[8,2,4096]{2,1,0:T(2,128)(2,1)S(1)}, bf16[8,2,4096]{2,1,0:T(2,128)(2,1)S(1)}, u32[]{:S(2)}, u32[]{:S(2)}) collective-permute-start(bf16[8,2,4096]{2,1,0:T(2,128)(2,1)S(1)} %all_to_all.10.near_ref), channel_id=1, source_target_pairs={{0,1},{1,0},{2,3},{3,2},{4,5},{5,4},{6,7},{7,6},{8,9},{9,8},{10,11... | collective-permute-start | bytes 393224 | tf_op jit(solution)/shard_map/ppermute | solution.py:376
  37.8 1.4 %collective-permute-start.1 = (bf16[16,4096]{1,0:T(8,128)(2,1)S(1)}, bf16[16,4096]{1,0:T(8,128)(2,1)S(1)}, u32[]{:S(2)}, u32[]{:S(2)}) collective-permute-start(bf16[16,4096]{1,0:T(8,128)(2,1)S(1)} %get-tuple-element.15), channel_id=1, source_target_pairs={{0,1},{1,0},{2,3},{3,2},{4,5},{5,4},{6,7},{7,6},{8,9},{9,8},{10,11... | collective-permute-start | bytes 393224 | tf_op jit(solution)/shard_map/ppermute | solution.py:381
where the time goes:
time: 50.7 us; the launch traced here: 50.2 us
  blocking collectives  24.4 us (48%)
  Pallas kernels  22.4 us (44%)
  waiting for transfers between devices  2.68 us (5%)
  between operations  0.66 us (1%)
    all_to_all x2, blocking collectives, exchange(): lax.all_to_all(array, 'exp', split_axis=0, concat_axis=0, tiled=True, axi...  24.4 us
    pallas_call x1, Pallas kernels, experts(): pl.pallas_call(experts_kernel, out_shape=(pltpu.VMEM((8, 128) if RET16 el...  19.4 us
    pallas_call x1, Pallas kernels, shards(): pl.pallas_call(attend_kernel, out_shape=(pltpu.VMEM(queries.shape, jnp.bf...  2.05 us
    ppermute x1, waiting for transfers between devices, shards(): far = lax.ppermute(near, 'exp', core_swap)  1.35 us
    ppermute x1, waiting for transfers between devices, shards(): taken = lax.ppermute(give, 'exp', core_swap)  1.33 us
  transfers between devices with their start and end apart: 2, of which 2 were waited for; matrix products, arithmetic and copies ran while one was open for 0% of the time, Pallas kernels for 0%

commit v1 on v0

--- a/solution.py
+++ b/solution.py
@@ -15,8 +15,6 @@
 QUAD = 4 * BLOCK
 SLOTS = 8
 
-FWD16 = False
-RET16 = False
 
 vmem = pl.BlockSpec(memory_space=pltpu.VMEM)
 smem = pl.BlockSpec(memory_space=pltpu.SMEM)
@@ -47,6 +45,7 @@
     attended_ref,
     outgoing_ref,
     mix_ref,
+    kept_gain_ref,
     list_ref,
 ):
     rows, width = queries_ref.shape
@@ -102,9 +101,6 @@
     attended_ref[...] = attended
 
     features = attended.astype(jnp.float32)
-    mean_square = jnp.mean(features * features, axis=1, keepdims=True)
-    normed = features * lax.rsqrt(mean_square + EPSILON) * gain_ref[...]
-    normed = normed.astype(jnp.bfloat16).astype(jnp.float32)
     places = outgoing_ref.shape[0]
     experts = flags_ref.shape[0]
     line = lax.broadcasted_iota(jnp.int32, (experts * CAP, 1), 0)
@@ -114,7 +110,7 @@
     mix = jnp.zeros(mix_ref.shape, jnp.float32)
     for r in range(rows):
         slots = [slot_of(ids_ref, r, k) for k in range(2)]
-        packed = packed + jnp.where((line == slots[0]) | (line == slots[1]), normed[r : r + 1, :], 0.0)
+        packed = packed + jnp.where((line == slots[0]) | (line == slots[1]), features[r : r + 1, :], 0.0)
         for k in range(2):
             mix = mix + jnp.where((mix_row == r) & (mix_slot == slots[k]), route_weights_ref[k, r], 0.0)
     packed = packed.astype(jnp.bfloat16)
@@ -122,6 +118,7 @@
         expert = place // (places // experts)
         outgoing_ref[place] = packed[expert * CAP : (expert + 1) * CAP, :]
     mix_ref[...] = mix
+    kept_gain_ref[...] = gain_ref[...]
 
 
 def list_blocks(flags_ref, list_ref, blocks):
@@ -174,6 +171,7 @@
     near_ref,
     far_ref,
     attended_ref,
+    gain_ref,
     gate_ref,
     up_ref,
     down_ref,
@@ -188,7 +186,6 @@
     attended_sem,
 ):
     blocks = gate_ref.shape[0] // BLOCK
-    core = lax.axis_index("exp") % 2
     chips = x_ref.shape[0] // (2 * CAP)
     half = chips * CAP
     ring_slots = ring_ref.shape[0]
@@ -208,8 +205,12 @@
     write = pltpu.make_async_copy(attended_ref, attended_out, attended_sem)
     write.start()
     for chip in range(chips):
-        x_ref[chip * CAP : (chip + 1) * CAP, :] = near_ref[2 * chip + core] if FWD16 else near_ref[chip]
-        x_ref[half + chip * CAP : half + (chip + 1) * CAP, :] = near_ref[2 * chip + 1 - core] if FWD16 else far_ref[chip]
+        x_ref[chip * CAP : (chip + 1) * CAP, :] = near_ref[chip]
+        x_ref[half + chip * CAP : half + (chip + 1) * CAP, :] = far_ref[chip]
+    features = x_ref[...].astype(jnp.float32)
+    mean_square = jnp.mean(features * features, axis=1, keepdims=True)
+    features = features * lax.rsqrt(mean_square + EPSILON)
+    x_ref[...] = (features * gain_ref[...]).astype(jnp.bfloat16)
     total_ref[...] = jnp.zeros_like(total_ref)
 
     def project(item, number):
@@ -251,13 +252,8 @@
 
     steps(project)
     steps(contract)
-    if RET16:
-        for chip in range(chips):
-            give_ref[2 * chip + core] = total_ref[chip * CAP : (chip + 1) * CAP, :].astype(jnp.bfloat16)
-            give_ref[2 * chip + 1 - core] = total_ref[half + chip * CAP : half + (chip + 1) * CAP, :].astype(jnp.bfloat16)
-    else:
-        keep_ref[...] = total_ref[0:half, :]
-        give_ref[...] = total_ref[half:, :].astype(jnp.bfloat16)
+    keep_ref[...] = total_ref[0:half, :]
+    give_ref[...] = total_ref[half:, :].astype(jnp.bfloat16)
     write.wait()
 
 
@@ -272,15 +268,17 @@
     experts = mix_ref.shape[1] // CAP
     share = returned_ref.shape[0] // experts
     mix = mix_ref[...]
-    total = jnp.zeros(out_ref.shape, jnp.float32)
-    for expert in range(experts):
-        value = returned_ref[expert * share].astype(jnp.float32)
-        for part in range(1, share):
-            value = value + returned_ref[expert * share + part].astype(jnp.float32)
-        for c in range(CAP):
-            slot = expert * CAP + c
-            total = total + mix[0:rows, slot : slot + 1] * value[c : c + 1, :]
-    out_ref[...] = total.astype(jnp.bfloat16)
+    high = mix.astype(jnp.bfloat16)
+    rest = mix - high.astype(jnp.float32)
+    middle = rest.astype(jnp.bfloat16)
+    low = (rest - middle.astype(jnp.float32)).astype(jnp.bfloat16)
+    weights = jnp.concatenate([high] * share + [middle] * share + [low] * share, axis=1)
+    parts = [
+        returned_ref[expert * share + part] for part in range(share) for expert in range(experts)
+    ]
+    values = jnp.concatenate(parts * 3, axis=0)
+    total = jnp.dot(weights, values, preferred_element_type=jnp.float32)
+    out_ref[...] = total[0:rows].astype(jnp.bfloat16)
 
 
 def ring_of(gate_weight):
@@ -293,17 +291,17 @@
     return pltpu.with_memory_space_constraint(array, pltpu.VMEM)
 
 
-def experts(listing, near, far, attended, gate_weight, up_weight, down_weight):
+def experts(listing, near, far, attended, gain, gate_weight, up_weight, down_weight):
     blocks, ring_shape = ring_of(gate_weight)
-    half, width = lax.axis_size("exp") // 2 * CAP, near.shape[2]
+    half, width = near.shape[0] * CAP, near.shape[2]
     return pl.pallas_call(
         experts_kernel,
         out_shape=(
-            pltpu.VMEM((8, 128) if RET16 else (half, width), jnp.float32),
-            pltpu.VMEM((half, CAP, width) if RET16 else (half, width), jnp.bfloat16),
+            pltpu.VMEM((half, width), jnp.float32),
+            pltpu.VMEM((half, width), jnp.bfloat16),
             jax.ShapeDtypeStruct(attended.shape, jnp.bfloat16),
         ),
-        in_specs=[smem, vmem, vmem, vmem, hbm, hbm, hbm],
+        in_specs=[smem] + [vmem] * 4 + [hbm] * 3,
         out_specs=(vmem, vmem, hbm),
         scratch_shapes=[
             pltpu.VMEM(ring_shape, jnp.bfloat16),
@@ -315,7 +313,14 @@
         ],
         compiler_params=pltpu.CompilerParams(vmem_limit_bytes=6 * 2**20 + 16 * half * width + 2 * math.prod(ring_shape)),
         name="experts",
-    )(pltpu.with_memory_space_constraint(listing, pltpu.SMEM), in_vmem(near), in_vmem(far), in_vmem(attended), gate_weight, up_weight, down_weight)
+    )(
+        pltpu.with_memory_space_constraint(listing, pltpu.SMEM),
+        in_vmem(near),
+        in_vmem(far),
+        in_vmem(attended),
+        in_vmem(gain),
+        *(pltpu.with_memory_space_constraint(weight, pltpu.HBM) for weight in (gate_weight, up_weight, down_weight)),
+    )
 
 
 def shards(
@@ -341,16 +346,17 @@
     core_swap = [(device, device ^ 1) for device in range(devices)]
 
     experts_number = active_blocks.shape[0]
-    attended, outgoing, mix, listing = pl.pallas_call(
+    attended, outgoing, mix, gain, listing = pl.pallas_call(
         attend_kernel,
         out_shape=(
             pltpu.VMEM(queries.shape, jnp.bfloat16),
-            pltpu.VMEM((devices if FWD16 else chips, CAP, width), jnp.bfloat16),
+            pltpu.VMEM((chips, CAP, width), jnp.bfloat16),
             pltpu.VMEM((8, experts_number * CAP), jnp.float32),
+            pltpu.VMEM((1, width), jnp.float32),
             pltpu.SMEM((1, gate_weight.shape[0] // BLOCK + 1), jnp.int32),
         ),
         in_specs=[smem] * 4 + [vmem] * 6,
-        out_specs=(vmem, vmem, vmem, smem),
+        out_specs=(vmem, vmem, vmem, vmem, smem),
         name="attend",
     )(
         lengths,
@@ -368,25 +374,18 @@
     def exchange(array):
         return lax.all_to_all(array, "exp", split_axis=0, concat_axis=0, tiled=True, axis_index_groups=same_core)
 
-    if FWD16:
-        near = lax.all_to_all(outgoing, "exp", split_axis=0, concat_axis=0, tiled=True)
-        far = near
-    else:
-        near = exchange(outgoing)
-        far = lax.ppermute(near, "exp", core_swap)
-    keep, give, attended = experts(listing, near, far, attended, gate_weight, up_weight, down_weight)
-    if RET16:
-        returned = lax.all_to_all(give, "exp", split_axis=0, concat_axis=0, tiled=True)
-    else:
-        taken = lax.ppermute(give, "exp", core_swap)
-        merged = pl.pallas_call(
-            merge_kernel,
-            out_shape=pltpu.VMEM((chips, CAP, width), jnp.bfloat16),
-            in_specs=[vmem, vmem],
-            out_specs=vmem,
-            name="merge",
-        )(in_vmem(keep), in_vmem(taken))
-        returned = exchange(merged)
+    near = exchange(outgoing)
+    far = lax.ppermute(near, "exp", core_swap)
+    keep, give, attended = experts(listing, near, far, attended, gain, gate_weight, up_weight, down_weight)
+    taken = lax.ppermute(give, "exp", core_swap)
+    merged = pl.pallas_call(
+        merge_kernel,
+        out_shape=pltpu.VMEM((chips, CAP, width), jnp.bfloat16),
+        in_specs=[vmem, vmem],
+        out_specs=vmem,
+        name="merge",
+    )(in_vmem(keep), in_vmem(taken))
+    returned = exchange(merged)
     expert_out = pl.pallas_call(
         combine_kernel,
         out_shape=jax.ShapeDtypeStruct(queries.shape, jnp.bfloat16),

time: 50.7 us -> 51.3 us (1.012); the launches traced: 50.2 us -> 52 us
  starting transfers between devices: 0.07 us -> 7.26 us
  Pallas kernels: 22.4 us -> 15.8 us
  blocking collectives: 24.4 us -> 26 us
    ppermute x1, starting transfers between devices: 0.07 us -> 7.26 us  [shards(): taken = lax.ppermute(give, 'exp', core_swap)]
    pallas_call x1, Pallas kernels: 19.4 us -> 13.1 us  [experts(): pl.pallas_call(experts_kernel, out_shape=(pltpu.VMEM((half, width), jnp.f...]
    all_to_all x2, blocking collectives: 24.4 us -> 26 us  [exchange(): lax.all_to_all(array, 'exp', split_axis=0, concat_axis=0, tiled=True, axi...]
where the time goes in v1:
time: 51.3 us; the launch traced here: 52 us
  blocking collectives  26 us (51%)
  Pallas kernels  15.8 us (31%)
  starting transfers between devices  7.26 us (14%)
  waiting for transfers between devices  2.33 us (5%)
  between operations  0.65 us (1%)
    all_to_all x2, blocking collectives, exchange(): lax.all_to_all(array, 'exp', split_axis=0, concat_axis=0, tiled=True, axi...  26 us
    pallas_call x1, Pallas kernels, experts(): pl.pallas_call(experts_kernel, out_shape=(pltpu.VMEM((half, width), jnp.f...  13.1 us
    ppermute x1, starting transfers between devices, shards(): taken = lax.ppermute(give, 'exp', core_swap)  7.26 us
    pallas_call x1, Pallas kernels, shards(): pl.pallas_call(attend_kernel, out_shape=(pltpu.VMEM(queries.shape, jnp.bf...  1.81 us
    ppermute x1, waiting for transfers between devices, shards(): far = lax.ppermute(near, 'exp', core_swap)  1.35 us
  transfers between devices with their start and end apart: 2, of which 2 were waited for; matrix products, arithmetic and copies ran while one was open for 0% of the time, Pallas kernels for 0%

profile of v1, /device:TPU:0, one launch (start us, length us, event | category | flops | bytes accessed | tf_op | source)
XLA Modules:
  0.0 52.0 jit_solution(8679078721877000497)
XLA Ops:
  0.6 1.8 %attend.1 = (bf16[4,4096]{1,0:T(4,128)(2,1)S(1)}, bf16[8,2,4096]{2,1,0:T(2,128)(2,1)S(1)}, f32[8,16]{1,0:T(8,128)S(1)}, f32[1,4096]{1,0:T(1,128)S(1)}, s32[1,33]{1,0:T(1,128)S(4)}) custom-call(s32[4]{0:T(128)} %lengths_ref.1, s32[2,4]{1,0:T(2,128)} %bitcast.4, f32[2,4]{1,0:T(2,128)} %bitcast.5, s32[8,64]{1,0:T(8,128)} %flags_ref.1, ...), custom_call_target="tpu_custom_call" | custom-call | tf_op jit(solution)/shard_map/attend/pallas_call | solution.py:349
  2.4 14.4 %all_to_all.10.near_ref = bf16[8,2,4096]{2,1,0:T(2,128)(2,1)S(1)} all-to-all(bf16[8,2,4096]{2,1,0:T(2,128)(2,1)S(1)} %get-tuple-element.11), channel_id=1, replica_groups={{0,2,4,6,8,10,12,14},{1,3,5,7,9,11,13,15},{16,18,20,22,24,26,28,30},{17..., dimensions={0} | all-to-all | bytes 262144 | tf_op jit(solution)/shard_map/all_to_all | solution.py:375
  16.8 0.0 collective-permute-start
  16.8 1.3 %collective-permute-done.far_ref = bf16[8,2,4096]{2,1,0:T(2,128)(2,1)S(1)} collective-permute-done((bf16[8,2,4096]{2,1,0:T(2,128)(2,1)S(1)}, bf16[8,2,4096]{2,1,0:T(2,128)(2,1)S(1)}, u32[]{:S(2)}, u32[]{:S(2)}) %collective-permute-start) | collective-permute-done | bytes 131104 | tf_op jit(solution)/shard_map/ppermute | solution.py:378
  18.2 13.1 %experts.1 = (f32[16,4096]{1,0:T(8,128)S(1)}, bf16[16,4096]{1,0:T(8,128)(2,1)S(1)}, bf16[4,4096]{1,0:T(4,128)(2,1)}) custom-call(s32[1,33]{1,0:T(1,128)S(4)} %get-tuple-element.10.list_ref, bf16[8,2,4096]{2,1,0:T(2,128)(2,1)S(1)} %all_to_all.10.near_ref, bf16[8,2,4096]{2,1,0:T(2,128)(2,1)S(1)} %collective-permute-done.far_ref, ...), custom_call_target="tpu_custom_call" | custom-call | tf_op jit(solution)/shard_map/experts/pallas_call | solution.py:297
  31.3 7.3 %collective-permute-start.1 = (bf16[16,4096]{1,0:T(8,128)(2,1)S(1)}, bf16[16,4096]{1,0:T(8,128)(2,1)S(1)}, u32[]{:S(2)}, u32[]{:S(2)}) collective-permute-start(bf16[16,4096]{1,0:T(8,128)(2,1)S(1)} %get-tuple-element.17), channel_id=1, source_target_pairs={{0,1},{1,0},{2,3},{3,2},{4,5},{5,4},{6,7},{7,6},{8,9},{9,8},{10,11... | collective-permute-start | bytes 393224 | tf_op jit(solution)/shard_map/ppermute | solution.py:380
  38.5 1.0 %collective-permute-done.1.taken_ref = bf16[16,4096]{1,0:T(8,128)(2,1)S(1)} collective-permute-done((bf16[16,4096]{1,0:T(8,128)(2,1)S(1)}, bf16[16,4096]{1,0:T(8,128)(2,1)S(1)}, u32[]{:S(2)}, u32[]{:S(2)}) %collective-permute-start.1) | collective-permute-done | bytes 131104 | tf_op jit(solution)/shard_map/ppermute | solution.py:380
  39.6 11.6 %all_to_all.11.returned_ref = bf16[8,2,4096]{2,1,0:T(2,128)(2,1)S(1)} all-to-all(bf16[8,2,4096]{2,1,0:T(2,128)(2,1)S(1)} %merge.1), channel_id=1, replica_groups={{0,2,4,6,8,10,12,14},{1,3,5,7,9,11,13,15},{16,18,20,22,24,26,28,30},{17..., dimensions={0} | all-to-all | bytes 262144 | tf_op jit(solution)/shard_map/all_to_all | solution.py:375
  51.2 0.9 %combine.1 = bf16[4,4096]{1,0:T(4,128)(2,1)} custom-call(f32[8,16]{1,0:T(8,128)S(1)} %get-tuple-element.15.mix_ref, bf16[8,2,4096]{2,1,0:T(2,128)(2,1)S(1)} %all_to_all.11.returned_ref), custom_call_target="tpu_custom_call" | custom-call | tf_op jit(solution)/shard_map/combine/pallas_call | solution.py:389
  (1 shorter events, 0.0 us)
Async XLA Ops:
  16.8 1.3 %collective-permute-start = (bf16[8,2,4096]{2,1,0:T(2,128)(2,1)S(1)}, bf16[8,2,4096]{2,1,0:T(2,128)(2,1)S(1)}, u32[]{:S(2)}, u32[]{:S(2)}) collective-permute-start(bf16[8,2,4096]{2,1,0:T(2,128)(2,1)S(1)} %all_to_all.10.near_ref), channel_id=1, source_target_pairs={{0,1},{1,0},{2,3},{3,2},{4,5},{5,4},{6,7},{7,6},{8,9},{9,8},{10,11... | collective-permute-start | bytes 393224 | tf_op jit(solution)/shard_map/ppermute | solution.py:378
  31.3 8.2 %collective-permute-start.1 = (bf16[16,4096]{1,0:T(8,128)(2,1)S(1)}, bf16[16,4096]{1,0:T(8,128)(2,1)S(1)}, u32[]{:S(2)}, u32[]{:S(2)}) collective-permute-start(bf16[16,4096]{1,0:T(8,128)(2,1)S(1)} %get-tuple-element.17), channel_id=1, source_target_pairs={{0,1},{1,0},{2,3},{3,2},{4,5},{5,4},{6,7},{7,6},{8,9},{9,8},{10,11... | collective-permute-start | bytes 393224 | tf_op jit(solution)/shard_map/ppermute | solution.py:380

commit v2 on v1

--- a/solution.py
+++ b/solution.py
@@ -229,29 +229,48 @@
             hidden_ref[item, :, s * BLOCK : (s + 1) * BLOCK] = hidden.astype(jnp.bfloat16)
         start(item + ring_slots, 0)
 
-    def contract(chunk, number):
-        item = pairs + chunk
-        settle(item)
-        total_ref[...] += jnp.dot(
-            hidden_ref[chunk, :, : number * BLOCK],
-            ring_ref[item % ring_slots, : number * BLOCK, :],
-            preferred_element_type=jnp.float32,
-        )
-        start(item + ring_slots, 0)
-
-    def steps(body):
-        def pair(step, carry):
-            body(step, 2)
-            return carry
-
-        lax.fori_loop(0, whole, pair, 0)
-
-        @pl.when(whole < pairs)
-        def _():
-            body(whole, 1)
-
-    steps(project)
-    steps(contract)
+    def contract(chunk, blocks_of):
+        items = [pairs + chunk + i for i in range(len(blocks_of))]
+        for item in items:
+            settle(item)
+        products = [
+            jnp.dot(
+                hidden_ref[chunk + i, :, : number * BLOCK],
+                ring_ref[items[i] % ring_slots, : number * BLOCK, :],
+                preferred_element_type=jnp.float32,
+            )
+            for i, number in enumerate(blocks_of)
+        ]
+        total_ref[...] += sum(products[1:], products[0])
+        for item in items:
+            start(item + ring_slots, 0)
+
+    def project_pair(item, carry):
+        project(item, 2)
+        return carry
+
+    def contract_wide(step, carry):
+        contract(2 * step, (2,) * 2)
+        return carry
+
+    def contract_pair(chunk, carry):
+        contract(chunk, (2,))
+        return carry
+
+    lax.fori_loop(0, whole, project_pair, 0)
+
+    @pl.when(whole < pairs)
+    def _():
+        project(whole, 1)
+
+    wide = jnp.maximum(whole - 1, 0) // 2
+    lax.fori_loop(0, wide, contract_wide, 0)
+    lax.fori_loop(2 * wide, whole, contract_pair, 0)
+
+    @pl.when(whole < pairs)
+    def _():
+        contract(whole, (1,))
+
     keep_ref[...] = total_ref[0:half, :]
     give_ref[...] = total_ref[half:, :].astype(jnp.bfloat16)
     write.wait()

time: 51.3 us -> 50.9 us (level)
  Pallas kernels: 15.8 us -> 23.6 us
  starting transfers between devices: 7.26 us -> 0.07 us
  blocking collectives: 26 us -> 24.4 us
    pallas_call x1, Pallas kernels: 13.1 us -> 20.9 us  [experts(): pl.pallas_call(experts_kernel, out_shape=(pltpu.VMEM((half, width), jnp.f...]
    ppermute x1, starting transfers between devices: 7.26 us -> 0.07 us  [shards(): taken = lax.ppermute(give, 'exp', core_swap)]
    all_to_all x2, blocking collectives: 26 us -> 24.4 us  [exchange(): lax.all_to_all(array, 'exp', split_axis=0, concat_axis=0, tiled=True, axi...]
where the time goes in v2:
time: 50.9 us; the launch traced here: 51.4 us
  blocking collectives  24.4 us (48%)
  Pallas kernels  23.6 us (46%)
  waiting for transfers between devices  2.68 us (5%)
  between operations  0.66 us (1%)
    all_to_all x2, blocking collectives, exchange(): lax.all_to_all(array, 'exp', split_axis=0, concat_axis=0, tiled=True, axi...  24.4 us
    pallas_call x1, Pallas kernels, experts(): pl.pallas_call(experts_kernel, out_shape=(pltpu.VMEM((half, width), jnp.f...  20.9 us
    pallas_call x1, Pallas kernels, shards(): pl.pallas_call(attend_kernel, out_shape=(pltpu.VMEM(queries.shape, jnp.bf...  1.81 us
    ppermute x1, waiting for transfers between devices, shards(): far = lax.ppermute(near, 'exp', core_swap)  1.35 us
    ppermute x1, waiting for transfers between devices, shards(): taken = lax.ppermute(give, 'exp', core_swap)  1.33 us
  transfers between devices with their start and end apart: 2, of which 2 were waited for; matrix products, arithmetic and copies ran while one was open for 0% of the time, Pallas kernels for 0%

profile of v2, /device:TPU:0, one launch (start us, length us, event | category | flops | bytes accessed | tf_op | source)
XLA Modules:
  0.0 51.4 jit_solution(4109696036098394905)
XLA Ops:
  0.6 1.8 %attend.1 = (bf16[4,4096]{1,0:T(4,128)(2,1)S(1)}, bf16[8,2,4096]{2,1,0:T(2,128)(2,1)S(1)}, f32[8,16]{1,0:T(8,128)S(1)}, f32[1,4096]{1,0:T(1,128)S(1)}, s32[1,33]{1,0:T(1,128)S(4)}) custom-call(s32[4]{0:T(128)} %lengths_ref.1, s32[2,4]{1,0:T(2,128)} %bitcast.4, f32[2,4]{1,0:T(2,128)} %bitcast.5, s32[8,64]{1,0:T(8,128)} %flags_ref.1, ...), custom_call_target="tpu_custom_call" | custom-call | tf_op jit(solution)/shard_map/attend/pallas_call | solution.py:368
  2.4 14.4 %all_to_all.10.near_ref = bf16[8,2,4096]{2,1,0:T(2,128)(2,1)S(1)} all-to-all(bf16[8,2,4096]{2,1,0:T(2,128)(2,1)S(1)} %get-tuple-element.11), channel_id=1, replica_groups={{0,2,4,6,8,10,12,14},{1,3,5,7,9,11,13,15},{16,18,20,22,24,26,28,30},{17..., dimensions={0} | all-to-all | bytes 262144 | tf_op jit(solution)/shard_map/all_to_all | solution.py:394
  16.8 0.0 collective-permute-start
  16.8 1.3 %collective-permute-done.far_ref = bf16[8,2,4096]{2,1,0:T(2,128)(2,1)S(1)} collective-permute-done((bf16[8,2,4096]{2,1,0:T(2,128)(2,1)S(1)}, bf16[8,2,4096]{2,1,0:T(2,128)(2,1)S(1)}, u32[]{:S(2)}, u32[]{:S(2)}) %collective-permute-start) | collective-permute-done | bytes 131104 | tf_op jit(solution)/shard_map/ppermute | solution.py:397
  18.2 20.9 %experts.1 = (f32[16,4096]{1,0:T(8,128)S(1)}, bf16[16,4096]{1,0:T(8,128)(2,1)S(1)}, bf16[4,4096]{1,0:T(4,128)(2,1)}) custom-call(s32[1,33]{1,0:T(1,128)S(4)} %get-tuple-element.10.list_ref, bf16[8,2,4096]{2,1,0:T(2,128)(2,1)S(1)} %all_to_all.10.near_ref, bf16[8,2,4096]{2,1,0:T(2,128)(2,1)S(1)} %collective-permute-done.far_ref, ...), custom_call_target="tpu_custom_call" | custom-call | tf_op jit(solution)/shard_map/experts/pallas_call | solution.py:316
  39.1 0.1 collective-permute-start.1
  39.2 1.3 %collective-permute-done.1.taken_ref = bf16[16,4096]{1,0:T(8,128)(2,1)S(1)} collective-permute-done((bf16[16,4096]{1,0:T(8,128)(2,1)S(1)}, bf16[16,4096]{1,0:T(8,128)(2,1)S(1)}, u32[]{:S(2)}, u32[]{:S(2)}) %collective-permute-start.1) | collective-permute-done | bytes 131104 | tf_op jit(solution)/shard_map/ppermute | solution.py:399
  40.6 10.0 %all_to_all.11.returned_ref = bf16[8,2,4096]{2,1,0:T(2,128)(2,1)S(1)} all-to-all(bf16[8,2,4096]{2,1,0:T(2,128)(2,1)S(1)} %merge.1), channel_id=1, replica_groups={{0,2,4,6,8,10,12,14},{1,3,5,7,9,11,13,15},{16,18,20,22,24,26,28,30},{17..., dimensions={0} | all-to-all | bytes 262144 | tf_op jit(solution)/shard_map/all_to_all | solution.py:394
  50.6 0.9 %combine.1 = bf16[4,4096]{1,0:T(4,128)(2,1)} custom-call(f32[8,16]{1,0:T(8,128)S(1)} %get-tuple-element.15.mix_ref, bf16[8,2,4096]{2,1,0:T(2,128)(2,1)S(1)} %all_to_all.11.returned_ref), custom_call_target="tpu_custom_call" | custom-call | tf_op jit(solution)/shard_map/combine/pallas_call | solution.py:408
  (1 shorter events, 0.0 us)
Async XLA Ops:
  16.8 1.3 %collective-permute-start = (bf16[8,2,4096]{2,1,0:T(2,128)(2,1)S(1)}, bf16[8,2,4096]{2,1,0:T(2,128)(2,1)S(1)}, u32[]{:S(2)}, u32[]{:S(2)}) collective-permute-start(bf16[8,2,4096]{2,1,0:T(2,128)(2,1)S(1)} %all_to_all.10.near_ref), channel_id=1, source_target_pairs={{0,1},{1,0},{2,3},{3,2},{4,5},{5,4},{6,7},{7,6},{8,9},{9,8},{10,11... | collective-permute-start | bytes 393224 | tf_op jit(solution)/shard_map/ppermute | solution.py:397
  39.1 1.4 %collective-permute-start.1 = (bf16[16,4096]{1,0:T(8,128)(2,1)S(1)}, bf16[16,4096]{1,0:T(8,128)(2,1)S(1)}, u32[]{:S(2)}, u32[]{:S(2)}) collective-permute-start(bf16[16,4096]{1,0:T(8,128)(2,1)S(1)} %get-tuple-element.17), channel_id=1, source_target_pairs={{0,1},{1,0},{2,3},{3,2},{4,5},{5,4},{6,7},{7,6},{8,9},{9,8},{10,11... | collective-permute-start | bytes 393224 | tf_op jit(solution)/shard_map/ppermute | solution.py:399

commit v3 on v1

--- a/solution.py
+++ b/solution.py
@@ -13,7 +13,7 @@
 EPSILON = 1e-05
 
 QUAD = 4 * BLOCK
-SLOTS = 8
+SLOTS = 7
 
 
 vmem = pl.BlockSpec(memory_space=pltpu.VMEM)

time: 51.3 us -> 50.4 us (0.982); the launches traced: 52 us -> 50.6 us
  blocking collectives: 26 us -> 24.6 us
  starting transfers between devices: 7.26 us -> 6.24 us
  Pallas kernels: 15.8 us -> 16.8 us
    all_to_all x2, blocking collectives: 26 us -> 24.6 us  [exchange(): lax.all_to_all(array, 'exp', split_axis=0, concat_axis=0, tiled=True, axi...]
    ppermute x1, starting transfers between devices: 7.26 us -> 6.23 us  [shards(): taken = lax.ppermute(give, 'exp', core_swap)]
    pallas_call x1, Pallas kernels: 13.1 us -> 14.1 us  [experts(): pl.pallas_call(experts_kernel, out_shape=(pltpu.VMEM((half, width), jnp.f...]
where the time goes in v3:
time: 50.4 us; the launch traced here: 50.6 us
  blocking collectives  24.6 us (49%)
  Pallas kernels  16.8 us (33%)
  starting transfers between devices  6.24 us (12%)
  waiting for transfers between devices  2.33 us (5%)
  between operations  0.65 us (1%)
    all_to_all x2, blocking collectives, exchange(): lax.all_to_all(array, 'exp', split_axis=0, concat_axis=0, tiled=True, axi...  24.6 us
    pallas_call x1, Pallas kernels, experts(): pl.pallas_call(experts_kernel, out_shape=(pltpu.VMEM((half, width), jnp.f...  14.1 us
    ppermute x1, starting transfers between devices, shards(): taken = lax.ppermute(give, 'exp', core_swap)  6.23 us
    pallas_call x1, Pallas kernels, shards(): pl.pallas_call(attend_kernel, out_shape=(pltpu.VMEM(queries.shape, jnp.bf...  1.81 us
    ppermute x1, waiting for transfers between devices, shards(): far = lax.ppermute(near, 'exp', core_swap)  1.35 us
  transfers between devices with their start and end apart: 2, of which 2 were waited for; matrix products, arithmetic and copies ran while one was open for 0% of the time, Pallas kernels for 0%

profile of v3, /device:TPU:0, one launch (start us, length us, event | category | flops | bytes accessed | tf_op | source)
XLA Modules:
  0.0 50.6 jit_solution(6986393264832018139)
XLA Ops:
  0.6 1.8 %attend.1 = (bf16[4,4096]{1,0:T(4,128)(2,1)S(1)}, bf16[8,2,4096]{2,1,0:T(2,128)(2,1)S(1)}, f32[8,16]{1,0:T(8,128)S(1)}, f32[1,4096]{1,0:T(1,128)S(1)}, s32[1,33]{1,0:T(1,128)S(4)}) custom-call(s32[4]{0:T(128)} %lengths_ref.1, s32[2,4]{1,0:T(2,128)} %bitcast.4, f32[2,4]{1,0:T(2,128)} %bitcast.5, s32[8,64]{1,0:T(8,128)} %flags_ref.1, ...), custom_call_target="tpu_custom_call" | custom-call | tf_op jit(solution)/shard_map/attend/pallas_call | solution.py:349
  2.4 14.4 %all_to_all.10.near_ref = bf16[8,2,4096]{2,1,0:T(2,128)(2,1)S(1)} all-to-all(bf16[8,2,4096]{2,1,0:T(2,128)(2,1)S(1)} %get-tuple-element.11), channel_id=1, replica_groups={{0,2,4,6,8,10,12,14},{1,3,5,7,9,11,13,15},{16,18,20,22,24,26,28,30},{17..., dimensions={0} | all-to-all | bytes 262144 | tf_op jit(solution)/shard_map/all_to_all | solution.py:375
  16.8 0.0 collective-permute-start
  16.8 1.3 %collective-permute-done.far_ref = bf16[8,2,4096]{2,1,0:T(2,128)(2,1)S(1)} collective-permute-done((bf16[8,2,4096]{2,1,0:T(2,128)(2,1)S(1)}, bf16[8,2,4096]{2,1,0:T(2,128)(2,1)S(1)}, u32[]{:S(2)}, u32[]{:S(2)}) %collective-permute-start) | collective-permute-done | bytes 131104 | tf_op jit(solution)/shard_map/ppermute | solution.py:378
  18.2 14.1 %experts.1 = (f32[16,4096]{1,0:T(8,128)S(1)}, bf16[16,4096]{1,0:T(8,128)(2,1)S(1)}, bf16[4,4096]{1,0:T(4,128)(2,1)}) custom-call(s32[1,33]{1,0:T(1,128)S(4)} %get-tuple-element.10.list_ref, bf16[8,2,4096]{2,1,0:T(2,128)(2,1)S(1)} %all_to_all.10.near_ref, bf16[8,2,4096]{2,1,0:T(2,128)(2,1)S(1)} %collective-permute-done.far_ref, ...), custom_call_target="tpu_custom_call" | custom-call | tf_op jit(solution)/shard_map/experts/pallas_call | solution.py:297
  32.3 6.2 %collective-permute-start.1 = (bf16[16,4096]{1,0:T(8,128)(2,1)S(1)}, bf16[16,4096]{1,0:T(8,128)(2,1)S(1)}, u32[]{:S(2)}, u32[]{:S(2)}) collective-permute-start(bf16[16,4096]{1,0:T(8,128)(2,1)S(1)} %get-tuple-element.17), channel_id=1, source_target_pairs={{0,1},{1,0},{2,3},{3,2},{4,5},{5,4},{6,7},{7,6},{8,9},{9,8},{10,11... | collective-permute-start | bytes 393224 | tf_op jit(solution)/shard_map/ppermute | solution.py:380
  38.5 1.0 %collective-permute-done.1.taken_ref = bf16[16,4096]{1,0:T(8,128)(2,1)S(1)} collective-permute-done((bf16[16,4096]{1,0:T(8,128)(2,1)S(1)}, bf16[16,4096]{1,0:T(8,128)(2,1)S(1)}, u32[]{:S(2)}, u32[]{:S(2)}) %collective-permute-start.1) | collective-permute-done | bytes 131104 | tf_op jit(solution)/shard_map/ppermute | solution.py:380
  39.5 10.2 %all_to_all.11.returned_ref = bf16[8,2,4096]{2,1,0:T(2,128)(2,1)S(1)} all-to-all(bf16[8,2,4096]{2,1,0:T(2,128)(2,1)S(1)} %merge.1), channel_id=1, replica_groups={{0,2,4,6,8,10,12,14},{1,3,5,7,9,11,13,15},{16,18,20,22,24,26,28,30},{17..., dimensions={0} | all-to-all | bytes 262144 | tf_op jit(solution)/shard_map/all_to_all | solution.py:375
  49.7 0.9 %combine.1 = bf16[4,4096]{1,0:T(4,128)(2,1)} custom-call(f32[8,16]{1,0:T(8,128)S(1)} %get-tuple-element.15.mix_ref, bf16[8,2,4096]{2,1,0:T(2,128)(2,1)S(1)} %all_to_all.11.returned_ref), custom_call_target="tpu_custom_call" | custom-call | tf_op jit(solution)/shard_map/combine/pallas_call | solution.py:389
  (1 shorter events, 0.0 us)
Async XLA Ops:
  16.8 1.3 %collective-permute-start = (bf16[8,2,4096]{2,1,0:T(2,128)(2,1)S(1)}, bf16[8,2,4096]{2,1,0:T(2,128)(2,1)S(1)}, u32[]{:S(2)}, u32[]{:S(2)}) collective-permute-start(bf16[8,2,4096]{2,1,0:T(2,128)(2,1)S(1)} %all_to_all.10.near_ref), channel_id=1, source_target_pairs={{0,1},{1,0},{2,3},{3,2},{4,5},{5,4},{6,7},{7,6},{8,9},{9,8},{10,11... | collective-permute-start | bytes 393224 | tf_op jit(solution)/shard_map/ppermute | solution.py:378
  32.3 7.2 %collective-permute-start.1 = (bf16[16,4096]{1,0:T(8,128)(2,1)S(1)}, bf16[16,4096]{1,0:T(8,128)(2,1)S(1)}, u32[]{:S(2)}, u32[]{:S(2)}) collective-permute-start(bf16[16,4096]{1,0:T(8,128)(2,1)S(1)} %get-tuple-element.17), channel_id=1, source_target_pairs={{0,1},{1,0},{2,3},{3,2},{4,5},{5,4},{6,7},{7,6},{8,9},{9,8},{10,11... | collective-permute-start | bytes 393224 | tf_op jit(solution)/shard_map/ppermute | solution.py:380
